TPU v7x, 256 devices: a whole 4x4x8 slice. The times are simulated.
256 devices in a mesh: vol: 8 (over z_lo, y), gz: 32 (over x, z_hi, core).
Axes of the slice: x: 4, y: 4, z: 8 (z_hi: 4, z_lo: 2; z = z_hi * 2 + z_lo), core: 2. Of those that a mesh axis runs over, the one named last changes fastest.
Arguments:
- volume: bfloat16 [8, 32, 128, 64, 128], P('vol', None, 'gz'), may hold values from -6 to 6
- kernel: bfloat16 [64, 32, 3, 3, 3], replicated, may hold values from -0.21875 to 0.21875
- cotangent: bfloat16 [8, 64, 64, 32, 64], P('vol', None, None, 'gz'), may hold values from -6 to 6
Outputs:
- features: bfloat16 [8, 64, 64, 32, 64], P('vol', None, None, 'gz')
- volume_grad: bfloat16 [8, 32, 128, 64, 128], P('vol', None, 'gz')
- kernel_grad: float32 [64, 32, 3, 3, 3], replicated
All inputs are finite; a program needn't handle non-finite values.
Results may differ from a plain program's by a relative error of at most 0.004.
Values may be sent and summed in bfloat16 or wider, within the bound.
A program may use at most 192 MiB of HBM per device.

v0:
```python
import jax
import jax.numpy as jnp
from jax import lax
from jax.sharding import PartitionSpec as P

FORWARD = ("NCDHW", "OIDHW", "NCDHW")
WEIGHTS = ("CNDHW", "IODHW", "CNDHW")


def from_behind(value, axis, steps):
    count = lax.axis_size(axis)
    leading, last = (max(0, -steps), min(count, count - steps))
    return lax.ppermute(value, axis, [(source, source + steps) for source in range(leading, last)])


def transpose_conv(grads, kernel):
    flipped = jnp.transpose(jnp.flip(kernel, (2, 3, 4)), (1, 0, 2, 3, 4))
    return lax.conv_general_dilated(
        grads,
        flipped,
        (1, 1, 1),
        ((2, 2), (2, 2), (2, 2)),
        lhs_dilation=(2, 2, 2),
        dimension_numbers=FORWARD,
        preferred_element_type=jnp.float32,
    )


def shards(volume, kernel, cotangent):
    planes = volume.shape[2]
    under_plane = from_behind(volume[:, :, planes - 1 :], "gz", 1)
    padded = jnp.pad(
        jnp.concatenate([under_plane, volume], axis=2), ((0, 0), (0, 0), (0, 0), (1, 0), (1, 0))
    )
    slab_out = lax.conv_general_dilated(
        padded,
        kernel,
        (2, 2, 2),
        "VALID",
        dimension_numbers=FORWARD,
        preferred_element_type=jnp.float32,
    ).astype(jnp.bfloat16)
    features = lax.all_to_all(slab_out, "gz", split_axis=3, concat_axis=2, tiled=True)
    slab_grad = lax.all_to_all(cotangent, "gz", split_axis=2, concat_axis=3, tiled=True)
    spread = transpose_conv(slab_grad, kernel)
    incoming = from_behind(spread[:, :, 0, 1:, 1:].astype(jnp.bfloat16), "gz", -1).astype(
        jnp.float32
    )
    inside = spread[:, :, 1:, 1:, 1:]
    inside = inside.at[:, :, planes - 1].add(incoming)
    volume_grad = inside.astype(jnp.bfloat16)
    partial_grad = lax.conv_general_dilated(
        padded,
        slab_grad,
        (1, 1, 1),
        "VALID",
        rhs_dilation=(2, 2, 2),
        dimension_numbers=WEIGHTS,
        preferred_element_type=jnp.float32,
    )
    volumes = volume.shape[0] * lax.axis_size("vol")
    summed = lax.psum(partial_grad, ("vol", "gz"))
    return (features, volume_grad, summed / volumes)


def solution(mesh):
    placed = (P("vol", None, "gz", None, None), P(), P("vol", None, None, "gz", None))
    return jax.shard_map(
        shards,
        mesh=mesh,
        in_specs=placed,
        out_specs=(P("vol", None, None, "gz", None), P("vol", None, "gz", None, None), P()),
        check_vma=False,
    )
```

profile of v0, /device:TPU:1, one launch (start us, length us, event | category | flops | bytes accessed | tf_op | source)
XLA Modules:
  0.0 523.7 jit_solution(16670843872921811112)
XLA Ops:
  7.2 0.0 copy-start
  7.2 1.1 slice.43
  8.3 6.3 %collective-permute-start = (bf16[1,32,1,64,128]{4,3,2,1,0:T(8,128)(2,1)S(1)}, bf16[1,32,1,64,128]{4,3,2,1,0:T(8,128)(2,1)}, u32[]{:S(2)}, u32[]{:S(2)}) collective-permute-start(bf16[1,32,1,64,128]{4,3,2,1,0:T(8,128)(2,1)S(1)} %slice.43), channel_id=1, source_target_pairs={{0,1},{1,2},{2,3},{3,4},{4,5},{5,6},{6,7},{7,8},{8,9},{9,10},{10,1... | collective-permute-start | bytes 1572872 | tf_op jit(solution)/shard_map/ppermute | solution.py:13
  14.6 1.9 copy.85
  16.5 1.6 reshape.92
  18.1 9.4 %all-to-all-start.1 = ((bf16[32,2,4096]{2,1,0:T(2,128)(2,1)}), bf16[32,2,4096]{2,1,0:T(2,128)(2,1)S(1)}, u32[]{:S(2)}, u32[]{:S(2)}) async-start(bf16[32,2,4096]{2,1,0:T(2,128)(2,1)} %reshape.92), calls=%async_computation.1 | async-start | bytes 1048576 | tf_op jit(solution)/shard_map/all_to_all | solution.py:44
  27.5 0.0 collective-permute-done
  27.5 1.1 constant_dynamic-update-slice_fusion.1
  28.6 2.0 constant_dynamic-update-slice_fusion
  30.6 22.3 %copy.75 = bf16[1,32,5,64,128]{1,0,4,3,2:T(2,128)(2,1)} copy(bf16[1,32,5,64,128]{4,3,2,1,0:T(8,128)(2,1)S(1)} %constant_dynamic-update-slice_fusion) | data formatting | bytes 5242880 | tf_op jit(solution)/shard_map/concatenate | solution.py:33
  52.8 7.8 %copy.81 = bf16[32,5,64,1,128]{2,0,4,1,3:T(8,128)(2,1)} copy(bf16[32,5,64,1,128]{4,2,1,0,3:T(8,128)(2,1)S(1)} %bitcast.57) | data formatting | bytes 5242880
  60.6 6.2 %pad.4.clone = bf16[32,5,64,1,144]{2,0,4,1,3:T(8,128)(2,1)} pad(bf16[32,5,64,1,128]{2,0,4,1,3:T(8,128)(2,1)} %copy.81, bf16[]{:T(256)} %constant.36), padding=0_0x0_0x0_0x0_0x1_15 | pad | bytes 5570562 | tf_op jit(solution)/shard_map/concatenate | solution.py:33
  66.8 0.0 copy-start.4
  66.8 15.7 %copy.63 = bf16[32,5,64,1,8,18]{0,4,5,2,1,3:T(8,128)(2,1)} copy(bf16[32,5,64,1,8,18]{2,0,5,4,1,3:T(8,128)(2,1)} %bitcast.55) | data formatting | bytes 5898240 | tf_op jit(solution)/shard_map/conv_general_dilated | solution.py:35
  82.5 1.7 slice.52
  84.2 0.0 copy-done
  84.2 0.0 copy-done.4
  84.2 10.1 %select_convert_fusion = bf16[2,32,8,9,64]{4,2,3,1,0:T(8,128)(2,1)S(1)} fusion(bf16[64,32,3,3,3]{0,1,4,3,2:T(8,128)(2,1)S(1)} %copy-done, bf16[32,5,64,1,7,2]{0,4,5,2,1,3:T(8,128)(2,1)S(1)} %slice.52, bf16[32,5,64,1,8,18]{0,4,5,2,1,3:T(8,128)(2,1)} %copy.63, pred[8,9]{0,1:T(8,128)(4,1)S(1)} %copy-done.4), kind=kOutput, calls=%fused_computation.11 | convolution fusion | flops 514719744 | bytes 3936328 | tf_op jit(solution)/shard_map/conv_general_dilated | solution.py:35
  94.3 0.2 copy.64
  94.5 0.1 slice_bitcast_fusion.3
  94.6 0.4 copy.86
  95.0 1.6 reshape.90
  96.6 0.0 all-to-all-done.1
  96.6 13.3 %all-to-all-start = ((bf16[32,2,4096]{2,1,0:T(2,128)(2,1)}), bf16[32,2,4096]{2,1,0:T(2,128)(2,1)}, u32[]{:S(2)}, u32[]{:S(2)}) async-start(bf16[32,2,4096]{2,1,0:T(2,128)(2,1)} %reshape.90), calls=%async_computation | async-start | bytes 1048576 | tf_op jit(solution)/shard_map/all_to_all | solution.py:43
  109.9 0.3 all-reduce.2.cloned.1.call-start
  110.2 0.7 reshape.93
  110.9 1.6 copy.82
  112.5 0.2 pad.6.clone
  112.7 0.5 copy.70
  113.2 0.3 fusion.33
  113.5 20.6 %fusion.12 = f32[5,65,8,18,32]{4,2,3,1,0:T(8,128)} fusion(bf16[64,32,3,3,3]{0,1,4,3,2:T(8,128)(2,1)S(1)} %copy-done, bf16[64,2,32,8,10]{0,3,4,2,1:T(8,128)(2,1)S(1)} %fusion.33), kind=kOutput, calls=%fused_computation.16 | convolution fusion | flops 509607936 | bytes 6756352 | tf_op jit(solution)/shard_map/conv_general_dilated | solution.py:18
  134.1 0.0 copy-start.3
  134.1 21.0 %copy.71 = f32[5,65,8,18,32]{1,4,3,2,0:T(8,128)} copy(f32[5,65,8,18,32]{4,2,3,1,0:T(8,128)} %fusion.12) | data formatting | bytes 11980800 | tf_op jit(solution)/shard_map/conv_general_dilated | solution.py:18
  155.1 0.0 copy-done.3
  155.1 9.7 %broadcast_select_fusion = f32[5,65,8,18,32]{1,4,3,2,0:T(8,128)} fusion(f32[5,65,8,18,32]{1,4,3,2,0:T(8,128)} %copy.71, pred[8,18]{1,0:T(8,128)(4,1)S(1)} %copy-done.3), kind=kLoop, calls=%fused_computation.7 | loop fusion | flops 1497600 | bytes 11980944 | tf_op jit(solution)/shard_map/conv_general_dilated | solution.py:18
  164.8 5.5 %fusion.24 = bf16[5,65,8,18,32]{1,4,3,2,0:T(8,128)(2,1)S(1)} fusion(f32[5,65,8,18,32]{1,4,3,2,0:T(8,128)} %copy.71, pred[8,18]{1,0:T(8,128)(4,1)S(1)} %copy-done.3), kind=kLoop, calls=%fused_computation.32 | loop fusion | flops 1497600 | bytes 8985744 | tf_op jit(solution)/shard_map/convert.1
  170.3 1.1 slice_bitcast_fusion.1
  171.3 0.4 slice_bitcast_fusion.2
  171.7 1.9 copy.72
  173.6 2.2 collective-permute-start.1
  175.8 13.6 %copy.76 = bf16[1,64,2,32,64]{1,0,4,3,2:T(2,128)(2,1)} copy(bf16[1,64,2,32,64]{4,1,2,3,0:T(8,128)(2,1)S(1)} %bitcast.59) | data formatting | bytes 1048576 | tf_op jit(solution)/shard_map/all_to_all | solution.py:44
  189.4 58.6 %fusion.25 = f32[64,32,3,3,3]{0,1,4,3,2:T(8,128)} fusion(bf16[1,32,5,64,128]{1,0,4,3,2:T(2,128)(2,1)} %copy.75, bf16[1,64,2,32,64]{1,0,4,3,2:T(2,128)(2,1)} %copy.76), kind=kOutput, calls=%fused_computation.35 | convolution fusion | flops 445931520 | bytes 3366912 | tf_op jit(solution)/shard_map/conv_general_dilated | solution.py:52
  248.1 0.0 all-reduce.2.cloned.1.call-update
  248.1 5.3 %slice_bitcast_fusion = f32[1,32,5,65,129]{3,1,4,2,0:T(8,128)S(1)} fusion(f32[5,65,1,144,32]{1,4,3,0,2:T(8,128)} %bitcast.54), kind=kLoop, calls=%fused_computation.5 | loop fusion | bytes 10732800 | tf_op jit(solution)/shard_map/conv_general_dilated | solution.py:18
  253.3 0.0 copy-start.2
  253.4 4.0 copy-done.2
  257.3 3.2 slice.56
  260.6 238.5 %all-reduce.2.cloned.1.call-done = f32[64,32,3,3,3]{0,1,4,3,2:T(8,128)} async-done(((f32[64,32,3,3,3]{0,1,4,3,2:T(8,128)}), f32[64,32,3,3,3]{0,1,4,3,2:T(8,128)}) %all-reduce.2.cloned.1.call-update) | async-done | bytes 221200 | tf_op jit(solution)/shard_map/psum | solution.py:62
  499.1 1.8 broadcast_multiply_fusion
  500.9 0.0 collective-permute-done.1
  500.9 2.5 copy.73
  503.4 3.2 fusion.7
  506.6 0.0 copy-start.1
  506.6 5.5 %copy.78 = bf16[1,32,4,64,128]{4,3,2,1,0:T(8,128)(2,1)} copy(bf16[1,32,4,64,128]{3,1,4,2,0:T(8,128)(2,1)} %fusion.7) | data formatting | bytes 4194304
  512.1 0.0 all-to-all-done
  512.1 2.3 reshape.91
  514.4 0.7 copy.66
  515.0 1.6 copy.77
  516.7 0.0 copy-done.1
  (1 shorter events, 0.0 us)
Async XLA Ops:
  7.2 77.0 %copy-start = (bf16[64,32,3,3,3]{0,1,4,3,2:T(8,128)(2,1)S(1)}, bf16[64,32,3,3,3]{0,1,4,3,2:T(8,128)(2,1)}, u32[]{:S(2)}) copy-start(bf16[64,32,3,3,3]{0,1,4,3,2:T(8,128)(2,1)} %param.6) | copy-start | bytes 331780
  8.3 19.2 %collective-permute-start = (bf16[1,32,1,64,128]{4,3,2,1,0:T(8,128)(2,1)S(1)}, bf16[1,32,1,64,128]{4,3,2,1,0:T(8,128)(2,1)}, u32[]{:S(2)}, u32[]{:S(2)}) collective-permute-start(bf16[1,32,1,64,128]{4,3,2,1,0:T(8,128)(2,1)S(1)} %slice.43), channel_id=1, source_target_pairs={{0,1},{1,2},{2,3},{3,4},{4,5},{5,6},{6,7},{7,8},{8,9},{9,10},{10,1... | collective-permute-start | bytes 1572872 | tf_op jit(solution)/shard_map/ppermute | solution.py:13
  18.1 78.5 %all-to-all-start.1 = ((bf16[32,2,4096]{2,1,0:T(2,128)(2,1)}), bf16[32,2,4096]{2,1,0:T(2,128)(2,1)S(1)}, u32[]{:S(2)}, u32[]{:S(2)}) async-start(bf16[32,2,4096]{2,1,0:T(2,128)(2,1)} %reshape.92), calls=%async_computation.1 | async-start | bytes 1048576 | tf_op jit(solution)/shard_map/all_to_all | solution.py:44
  66.8 17.4 %copy-start.4 = (pred[8,9]{0,1:T(8,128)(4,1)S(1)}, pred[8,9]{0,1:T(8,128)(4,1)}, u32[]{:S(2)}) copy-start(pred[8,9]{0,1:T(8,128)(4,1)} %constant.44) | copy-start | bytes 220
  96.6 415.5 %all-to-all-start = ((bf16[32,2,4096]{2,1,0:T(2,128)(2,1)}), bf16[32,2,4096]{2,1,0:T(2,128)(2,1)}, u32[]{:S(2)}, u32[]{:S(2)}) async-start(bf16[32,2,4096]{2,1,0:T(2,128)(2,1)} %reshape.90), calls=%async_computation | async-start | bytes 1048576 | tf_op jit(solution)/shard_map/all_to_all | solution.py:43
  109.9 389.2 %all-reduce.2.cloned.1.call-start = ((), (), s32[]{:S(2)}) async-start(), calls=%async_computation.2 | async-start | bytes 884736 | tf_op jit(solution)/shard_map/psum | solution.py:62
  134.1 21.0 %copy-start.3 = (pred[8,18]{1,0:T(8,128)(4,1)S(1)}, pred[8,18]{1,0:T(8,128)(4,1)}, u32[]{:S(2)}) copy-start(pred[8,18]{1,0:T(8,128)(4,1)} %constant.45) | copy-start | bytes 436
  173.6 327.3 %collective-permute-start.1 = (bf16[1,32,64,128]{3,2,1,0:T(8,128)(2,1)}, bf16[1,32,64,128]{3,2,1,0:T(8,128)(2,1)}, u32[]{:S(2)}, u32[]{:S(2)}) collective-permute-start(bf16[1,32,64,128]{3,2,1,0:T(8,128)(2,1)} %copy.72), channel_id=1, source_target_pairs={{1,0},{2,1},{3,2},{4,3},{5,4},{6,5},{7,6},{8,7},{9,8},{10,9},{11,1... | collective-permute-start | bytes 1572872 | tf_op jit(solution)/shard_map/ppermute | solution.py:13
  253.3 4.0 copy-start.2
  506.6 10.1 %copy-start.1 = (bf16[64,32,3,3,3]{0,1,4,3,2:T(8,128)(2,1)S(1)}, bf16[64,32,3,3,3]{0,1,4,3,2:T(8,128)(2,1)}, u32[]{:S(2)}) copy-start(bf16[64,32,3,3,3]{0,1,4,3,2:T(8,128)(2,1)} %param.6) | copy-start | bytes 331780
Sparse Core Ops, SparseCore 0:
  248.2 250.8 all-reduce.1
where the time goes:
time: 529 us; the launch traced here: 524 us
  waiting for transfers between devices  239 us (45%)
  local copies, waits for them, and re-layouts  130 us (25%)
  matrix products  89.3 us (17%)
  starting transfers between devices  31.5 us (6%)
  other arithmetic  20.4 us (4%)
  between operations  14.4 us (3%)
    psum x1, waiting for transfers between devices, shards(): summed = lax.psum(partial_grad, ('vol', 'gz'))  239 us
    conv_general_dilated x1, matrix products, shards(): lax.conv_general_dilated(padded, slab_grad, (1, 1, 1), 'VALID', rhs_dilat...  58.6 us
    concatenate x3, local copies, waits for them, and re-layouts, shards(): jnp.concatenate([under_plane, volume], axis=2)  30.5 us
    unnamed x20, local copies, waits for them, and re-layouts  29.7 us
    conv_general_dilated x4, local copies, waits for them, and re-layouts, transpose_conv(): lax.conv_general_dilated(grads, flipped, (1, 1, 1), ((2, 2), (2, 2), (2,...  26.8 us
    conv_general_dilated x1, matrix products, transpose_conv(): lax.conv_general_dilated(grads, flipped, (1, 1, 1), ((2, 2), (2, 2), (2,...  20.6 us
    conv_general_dilated x2, local copies, waits for them, and re-layouts, shards(): lax.conv_general_dilated(padded, kernel, (2, 2, 2), 'VALID', dimension_nu...  17.4 us
    all_to_all x2, local copies, waits for them, and re-layouts, shards(): lax.all_to_all(cotangent, 'gz', split_axis=2, concat_axis=3, tiled=True)  13.8 us
  transfers between devices with their start and end apart: 5, of which 1 were waited for; matrix products, arithmetic and copies ran while one was open for 44% of the time, Pallas kernels for 0%

commit v1 on v0

v1 whole, which is shorter than its diff:
```python
import functools

import jax
import jax.numpy as jnp
import numpy as np
from jax import lax
from jax.experimental import pallas as pl
from jax.experimental.pallas import tpu as pltpu
from jax.sharding import PartitionSpec as P

MESH = pl.DeviceIdType.MESH
BF = jnp.bfloat16
F32 = jnp.float32

CI, CO, SLABS, BANDS = 32, 64, 32, 4
QB = 5 * CO

BACK = ((0, 0), (0, 2), (2, 2), (2, 0), (0, 1), (2, 1), (1, 2), (1, 0), (1, 1))
FRONT = ((1, 0), (1, 1), (1, 2), (2, 0), (2, 1), (2, 2), (0, 0), (0, 1), (0, 2))
TAPS = tuple((a, b, e) for e in range(3) for a in (1, 2, 0) for b in range(3))
GROUPS = 7


def one_hot(rows, columns, test):
    row, column = np.meshgrid(np.arange(rows), np.arange(columns), indexing="ij")
    return np.asarray(test(row, column), np.float32).astype(jnp.bfloat16)


def pair_pick(row, column):
    half, o, p = column // 256, column // 16 % 16, column % 16
    return (row % 16 == o) & (p == 2 * (row // 16) + half)


def even_pick(row, column):
    o, p = column // 16 % 16, column % 16
    return (row % 16 == o) & (p == 2 * (row // 16))


def unpick(row, column):
    half, slab, o = column // 128, column // 16 % 8, column % 16
    return (row // 16 == o) & (row % 16 == 2 * slab + half)


def place(row, column):
    ql, c, yl = row // 256, row // 8 % 32, row % 8
    b, channel = column // 32, column % 32
    return (b < 3) & (c == channel) & (yl == 2 * ql + b - 1)


def spread_x(row, column):
    zz, x = row // 128, row % 128
    e, half, r = column // 128, column // 64 % 2, column % 64
    return (zz == half) & (x == 2 * r + e - 1)


def weave_x(row, column):
    parity, zz, r = row // 128, row // 64 % 2, row % 64
    return (zz == column // 128) & (column % 128 == 2 * r + parity)


def later_planes(high, row, column):
    kind, lane = column // 128, column % 128
    shift = np.where(kind == 1, 0, 1)
    valid = (lane % 64 + shift) < 64
    lane = lane + shift
    later = np.where(lane % 128 < 64, lane + 64, 128 + lane - (0 if high else 64))
    return valid & (row == np.where(kind == 2, lane, later))


def halves(row, column):
    return (column % 64 == row) & ((column // 64 == 0) | (column // 64 == 3))


def join(upper, row, column):
    even = (row == column) | (row == 128 + 64 * upper + column)
    odd = row == column - 64
    return np.where(column < 64, even, (column // 64 == 2) & odd)


def sum_band(row, column):
    return row // 8 == column


CONSTANTS = (
    ("halves", one_hot(64, 256, halves)),
    ("pairs", one_hot(128, 512, pair_pick)),
    ("evens", one_hot(128, 512, even_pick)),
    ("place", one_hot(5 * 256, 128, place)),
    ("place_t", np.ascontiguousarray(one_hot(5 * 256, 128, place).T)),
    ("spread", one_hot(256, 384, spread_x)),
    ("later_lo", one_hot(256, 384, functools.partial(later_planes, False))),
    ("later_hi", one_hot(256, 384, functools.partial(later_planes, True))),
    ("bands", one_hot(1024, 128, sum_band)),
    ("weave", one_hot(256, 256, weave_x)),
    ("join_lo", one_hot(256, 256, functools.partial(join, 0))),
    ("join_hi", one_hot(256, 256, functools.partial(join, 1))),
    ("unpick", one_hot(256, 256, unpick)),
)
NC = len(CONSTANTS)


def dot(a, b):
    return jnp.dot(a, b, preferred_element_type=F32)


def dot_nt(a, b):
    return lax.dot_general(a, b, (((1,), (1,)), ((), ())), preferred_element_type=F32)


def kernel(*refs):
    (vol_in, w_in, cot_in), refs = refs[:3], refs[3:]
    const_in, refs = refs[:NC], refs[NC:]
    (feat_out, vgrad_out, kgrad_out), refs = refs[:3], refs[3:]
    const, refs = refs[:NC], refs[NC:]
    k = {name: ref for (name, _), ref in zip(CONSTANTS, const)}
    (vol, w, cot, feat, vgrad, kgrad, cs, cr, fs, rf, wa, tc, tt_oo, tt_oe, tt_e, vc, c4,
     carry, dh, dl, p1, r1, s1, r2, s2, r3, s3, r4, r5,
     in_sem, const_sem, out_sem, cot_send, cot_recv, ft_send, ft_recv,
     a_send, a_recv, z_send, z_recv, x_send, x_recv, zz_send, zz_recv, aa_send, aa_recv) = refs

    mv, mg = lax.axis_index("vol"), lax.axis_index("gz")
    y, z_lo = mv % 4, mv // 4
    core, z_hi, x = mg % 2, mg // 2 % 4, mg // 8
    mine, z = y * 2 + core, z_hi * 2 + z_lo

    barrier = pltpu.get_barrier_semaphore()

    def greet(v, g):
        pl.semaphore_signal(barrier, inc=1, device_id=(v, g), device_id_type=MESH)

    def greet_slab(i, _):
        greet(mv, (mg + i) % SLABS)
        return 0

    lax.fori_loop(1, SLABS, greet_slab, 0)
    for step in range(1, 4):
        for other in range(2):
            greet(z_lo * 4 + (y + step) % 4, mg - core + other)
    for other in range(4):
        greet((1 - z_lo) * 4 + y, x * 8 + other * 2 + core)

    load_cot = pltpu.make_async_copy(cot_in, cot, in_sem.at[0])
    load_w = pltpu.make_async_copy(w_in, w, in_sem.at[1])
    load_vol = pltpu.make_async_copy(vol_in, vol, in_sem.at[2])
    loads = {
        name: pltpu.make_async_copy(const_in[i], const[i], const_sem.at[i])
        for i, (name, _) in enumerate(CONSTANTS)
    }
    load_cot.start()
    for name in ("halves", "pairs", "evens"):
        loads[name].start()
    load_w.start()
    load_vol.start()
    for name in list(loads)[3:]:
        loads[name].start()

    cs[SLABS, 64:96, :] = jnp.zeros((32, 128), BF)
    rf[0, 64:96, :] = jnp.zeros((32, 128), BF)
    c4[BANDS, 1024:1280, 128:256] = jnp.zeros((256, 128), BF)
    dh[384:448, 768:1024] = jnp.zeros((64, 256), BF)
    dl[384:448, 768:1024] = jnp.zeros((64, 256), BF)
    p1[:, GROUPS, :, :] = jnp.zeros((8, 8, 128), F32)
    carry[...] = jnp.zeros((2, 64, 128), F32)

    load_cot.wait()
    for name in ("halves", "pairs", "evens"):
        loads[name].wait()

    def pack(m, _):
        wide = []
        for g in range(4):
            block = cot[16 * g : 16 * g + 16, pl.ds(16 * m, 16), :].reshape(256, 64)
            wide.append(dot(block, k["halves"][...]).astype(BF))
        for g in range(4):
            both = jnp.concatenate([wide[g][:, :128], wide[g][:, 128:]], axis=0)
            two = dot(k["pairs"][...], both).astype(BF)
            cs[pl.ds(8 * m + 1, 8), 16 * g : 16 * g + 16, :] = two.reshape(8, 16, 128)
        for g in range(2):
            both = jnp.concatenate([wide[g][:, :128], wide[g + 2][:, 128:]], axis=0)
            two = dot(k["evens"][...], both).astype(BF)
            cs[pl.ds(8 * m, 8), 64 + 16 * g : 80 + 16 * g, :] = two.reshape(8, 16, 128)
        return 0

    lax.fori_loop(0, 4, pack, 0)

    pl.semaphore_wait(barrier, 41)

    def cot_copy(to, slot):
        return pltpu.make_async_remote_copy(
            src_ref=cs.at[to + 1], dst_ref=cr.at[slot],
            send_sem=cot_send.at[to], recv_sem=cot_recv.at[slot],
            device_id=(mv, to), device_id_type=MESH)

    def send_cot(i, _):
        cot_copy((mg + i) % SLABS, mg).start()
        return 0

    lax.fori_loop(1, SLABS, send_cot, 0)
    cr[mg] = cs[mg + 1]

    load_w.wait()
    wa[...] = jnp.zeros((128, 640), F32)
    for b in range(3):
        for i in range(0, 10, 2):
            (a, e), rows = BACK[i], slice(32 * b, 32 * b + 32)
            first = w[a, b, e].astype(F32)
            if i + 1 < 9:
                a, e = BACK[i + 1]
                second = w[a, b, e].astype(F32)
            else:
                second = jnp.zeros((32, 64), F32)
            wa[rows, 64 * i : 64 * i + 128] = jnp.concatenate([first, second], axis=1)
    for name in ("place", "place_t"):
        loads[name].wait()
    taps = wa[...]
    back = taps.astype(BF)
    front = jnp.transpose(taps).astype(BF)
    for ql in range(5):
        t = dot(k["place"][256 * ql : 256 * ql + 256, :], back).astype(BF)
        tt_oo[:, 256 * ql : 256 * ql + 256] = t[:, 0:256]
        tt_oe[:, 128 * ql : 128 * ql + 128] = t[:, 256:384]
        tt_e[0:256, 128 * ql : 128 * ql + 128] = t[:, 384:512]
        tt_e[256:512, 128 * ql : 128 * ql + 128] = t[:, 512:640]
        t = dot(front, k["place_t"][:, 256 * ql : 256 * ql + 256]).astype(BF)
        for i, pair in enumerate(FRONT):
            j = BACK.index(pair)
            tc[64 * ql : 64 * ql + 64, 256 * i : 256 * i + 256] = t[64 * j : 64 * j + 64, :]

    load_vol.wait()
    loads["spread"].wait()

    def split_x(n, _):
        for parity in range(2):
            both = jnp.concatenate(
                [vol[:, 2 * zz + parity, pl.ds(16 * n, 16), :].reshape(512, 128) for zz in range(2)],
                axis=1)
            s = dot(both, k["spread"][...]).reshape(CI, 16, 384)
            for h in range(2):
                part = s[:, 8 * h : 8 * h + 8, :].reshape(256, 384).astype(BF)
                for e in range(3):
                    row = (3 * parity + e) * 256
                    vc[n, row : row + 256, 128 * h : 128 * h + 128] = part[:, 128 * e : 128 * e + 128]
        return 0

    lax.fori_loop(0, BANDS, split_x, 0)

    lane = lax.broadcasted_iota(jnp.int32, (256, 128), 1)

    def ft_copy(to, slot):
        return pltpu.make_async_remote_copy(
            src_ref=fs.at[to], dst_ref=rf.at[slot + 1],
            send_sem=ft_send.at[to], recv_sem=ft_recv.at[slot],
            device_id=(mv, to), device_id_type=MESH)

    def forward(n, _):
        f01 = dot(tc[:, :1536], vc[n])
        f12 = dot(tc[:, 1536:], vc[n, 768:1536, :])
        for h in range(2):
            a, b = f01[:, 128 * h : 128 * h + 128], f12[:, 128 * h : 128 * h + 128]
            own = jnp.concatenate([a[0:64] + carry[0], a[64:256]], axis=0)
            late = jnp.concatenate([b[0:64] + carry[1], b[64:256]], axis=0)
            carry[0], carry[1] = a[256:320], b[256:320]
            swapped = pltpu.roll(late, 64, 1)
            total = (own + jnp.where(lane >= 64, swapped, 0.0)).astype(BF)
            for ql in range(4):
                q = 8 * n + 4 * h + ql
                low, high = swapped[64 * ql : 64 * ql + 32], late[64 * ql + 32 : 64 * ql + 64]
                fs[q, 0:64, :] = total[64 * ql : 64 * ql + 64]
                fs[q, 64:96, :] = jnp.where(lane[0:32] < 64, low, high).astype(BF)
        return 0

    lax.fori_loop(0, BANDS, forward, 0)

    def send_ft(i, _):
        ft_copy((mg + i) % SLABS, mg).start()
        return 0

    lax.fori_loop(1, SLABS, send_ft, 0)
    rf[mg + 1] = fs[mg]

    def wait_cot(i, _):
        cot_copy((mg + i) % SLABS, (mg + i) % SLABS).wait_recv()
        return 0

    lax.fori_loop(1, SLABS, wait_cot, 0)
    loads["later_lo"].wait()
    loads["later_hi"].wait()

    def forms(n, _):
        blocks = [cr[8 * n + i] for i in range(8)]
        for part, name in ((0, "later_lo"), (1, "later_hi")):
            rows = jnp.concatenate(
                [jnp.concatenate([x_[32 * part : 32 * part + 32], x_[64:96]], axis=1) for x_ in blocks],
                axis=0)
            made = dot(rows, k[name][...]).astype(BF)
            for i in range(8):
                h, ql = i // 4, i % 4
                new = made[32 * i : 32 * i + 32]
                four = (new[:, 0:128], new[:, 128:256], blocks[i][32 * part : 32 * part + 32], new[:, 256:384])
                for v, value in enumerate(four):
                    row = 64 * v + 32 * part
                    c4[n + 1, 256 * ql + row : 256 * ql + row + 32, 128 * h : 128 * h + 128] = value
                    if ql == 0:
                        row += 1024
                        c4[n + h, row : row + 32, 128 * (1 - h) : 128 * (2 - h)] = value
        return 0

    lax.fori_loop(0, BANDS, forms, 0)

    yl = lax.broadcasted_iota(jnp.int32, (64, 256), 1) % 8
    for e in range(3):
        g_odd, g_even = None, None
        for n in range(BANDS):
            later = jnp.concatenate(
                [c4[n + 1, 256 * ql + 64 : 256 * ql + 192, :] for ql in range(5)], axis=0)
            own = jnp.concatenate(
                [c4[n + 1, 256 * ql + 128 : 256 * ql + 192, :] for ql in range(5)], axis=0)
            odd = dot_nt(later, vc[n, 256 * (3 + e) : 256 * (4 + e), :])
            even = dot_nt(own, vc[n, 256 * e : 256 * (e + 1), :])
            g_odd = odd if g_odd is None else g_odd + odd
            g_even = even if g_even is None else g_even + even
        for i in range(3):
            if i == 0:
                g = [g_even[64 * ql : 64 * ql + 64] for ql in range(5)]
            else:
                start = 64 if i == 1 else 0
                g = [g_odd[128 * ql + start : 128 * ql + start + 64] for ql in range(5)]
            d0 = jnp.where(yl == 1, g[1], jnp.where(yl == 3, g[2], jnp.where(
                yl == 5, g[3], jnp.where(yl == 7, g[4], 0.0))))
            rest = jnp.where(yl < 2, g[0], jnp.where(yl < 4, g[1], jnp.where(yl < 6, g[2], g[3])))
            d1, d2 = jnp.where(yl % 2 == 0, rest, 0.0), jnp.where(yl % 2 == 1, rest, 0.0)
            for b, d in enumerate((d0, d1, d2)):
                group, slot = divmod(9 * e + 3 * i + b, 4)
                at = (slice(64 * group, 64 * group + 64), slice(256 * slot, 256 * slot + 256))
                top = d.astype(BF)
                dh[at] = top
                dl[at] = (d - top.astype(F32)).astype(BF)
    loads["bands"].wait()
    packed = dot(dh[...], k["bands"][...]) + dot(dl[...], k["bands"][...])
    for g in range(GROUPS):
        for m in range(8):
            p1[m, g] = packed[64 * g + 8 * m : 64 * g + 8 * m + 8]

    def a_copy(source, target, send, recv, to, slot):
        return pltpu.make_async_remote_copy(
            src_ref=source, dst_ref=target.at[slot], send_sem=send.at[to], recv_sem=recv.at[slot],
            device_id=(z_lo * 4 + to // 2, mg - core + to % 2), device_id_type=MESH)

    def z_copy(source, target, send, recv, to, slot):
        return pltpu.make_async_remote_copy(
            src_ref=source, dst_ref=target.at[slot], send_sem=send.at[to], recv_sem=recv.at[slot],
            device_id=(to % 2 * 4 + y, x * 8 + to // 2 * 2 + core), device_id_type=MESH)

    def x_copy(to, slot):
        return pltpu.make_async_remote_copy(
            src_ref=s2, dst_ref=r3.at[slot], send_sem=x_send.at[to], recv_sem=x_recv.at[slot],
            device_id=(mv, to * 8 + z_hi * 2 + core), device_id_type=MESH)

    loads["weave"].wait()

    def backward(n):
        c = [c4[n + 1, 256 * ql : 256 * ql + 256, :] for ql in range(5)]
        oo = dot(tt_oo[...], c4[n + 1])
        oe = dot(tt_oe[...], jnp.concatenate([v[64:192] for v in c], axis=0))
        ev = dot(tt_e[...], jnp.concatenate([v[128:256] for v in c], axis=0))
        for parity, (at_even, at_odd) in enumerate(((ev[256:512], ev[0:256]), (oe, oo))):
            even, odd = at_even.astype(BF), at_odd.astype(BF)
            parts = []
            for h in range(2):
                lanes = slice(128 * h, 128 * h + 128)
                both = jnp.concatenate([even[:, lanes], odd[:, lanes]], axis=1)
                parts.append(dot(both, k["weave"][...]).reshape(CI, 8, 256))
            out = jnp.concatenate(parts, axis=1).astype(BF)
            for zz in range(2):
                vgrad[:, 2 * zz + parity, 16 * n : 16 * n + 16, :] = out[:, :, 128 * zz : 128 * zz + 128]

    def each(count, me, act):
        for i in range(1, count):
            act((me + i) % count)

    each(8, mine, lambda to: a_copy(p1.at[to], r1, a_send, a_recv, to, mine).start())
    r1[mine] = p1[mine]
    backward(0)
    each(8, mine, lambda to: a_copy(p1.at[to], r1, a_send, a_recv, to, to).wait_recv())
    s1[...] = functools.reduce(jnp.add, [r1[i] for i in range(8)])

    each(8, z, lambda to: z_copy(s1.at[to], r2, z_send, z_recv, to, z).start())
    r2[z] = s1[z]
    backward(1)
    each(8, z, lambda to: z_copy(s1.at[to], r2, z_send, z_recv, to, to).wait_recv())
    s2[...] = functools.reduce(jnp.add, [r2[i] for i in range(8)])

    each(4, x, lambda to: x_copy(to, x).start())
    r3[x] = s2[...]
    backward(2)
    each(4, x, lambda to: x_copy(to, to).wait_recv())
    s3[...] = functools.reduce(jnp.add, [r3[i] for i in range(4)]) * 0.125

    each(8, z, lambda to: z_copy(s3, r4, zz_send, zz_recv, to, z).start())
    r4[z] = s3[...]
    backward(3)
    store_vgrad = pltpu.make_async_copy(vgrad, vgrad_out, out_sem.at[0])
    store_vgrad.start()
    each(8, z, lambda to: z_copy(s3, r4, zz_send, zz_recv, to, to).wait_recv())

    each(8, mine, lambda to: a_copy(r4, r5, aa_send, aa_recv, to, mine).start())
    r5[mine] = r4[...]

    def wait_ft(i, _):
        ft_copy((mg + i) % SLABS, (mg + i) % SLABS).wait_recv()
        return 0

    lax.fori_loop(1, SLABS, wait_ft, 0)
    for name in ("join_lo", "join_hi", "unpick"):
        loads[name].wait()

    def unpack(m, _):
        for g in range(4):
            two = rf[pl.ds(8 * m + 1, 8), 16 * g : 16 * g + 16, :].reshape(128, 128)
            row = 64 + 16 * (g % 2)
            one = rf[pl.ds(8 * m, 8), row : row + 16, :].reshape(128, 128)
            summed = k["join_hi"] if g >= 2 else k["join_lo"]
            planes = dot(jnp.concatenate([two, one], axis=1), summed[...]).astype(BF)
            planes = jnp.concatenate([planes[:, 0:128], planes[:, 128:256]], axis=0)
            rows = dot(k["unpick"][...], planes)[:, 0:64].astype(BF)
            feat[16 * g : 16 * g + 16, pl.ds(16 * m, 16), :] = rows.reshape(16, 16, 64)
        return 0

    lax.fori_loop(0, 4, unpack, 0)
    store_feat = pltpu.make_async_copy(feat, feat_out, out_sem.at[1])
    store_feat.start()

    each(8, mine, lambda to: a_copy(r4, r5, aa_send, aa_recv, to, to).wait_recv())
    for g in range(GROUPS):
        total = jnp.transpose(r5[:, g].reshape(64, 128))
        for slot in range(4):
            if 4 * g + slot < len(TAPS):
                kgrad[TAPS[4 * g + slot]] = total[32 * slot : 32 * slot + 32]
    store_kgrad = pltpu.make_async_copy(kgrad, kgrad_out, out_sem.at[2])
    store_kgrad.start()

    def sent(i, _):
        to = (mg + i) % SLABS
        cot_copy(to, mg).wait_send()
        ft_copy(to, mg).wait_send()
        return 0

    lax.fori_loop(1, SLABS, sent, 0)
    each(8, mine, lambda to: a_copy(p1.at[to], r1, a_send, a_recv, to, mine).wait_send())
    each(8, z, lambda to: z_copy(s1.at[to], r2, z_send, z_recv, to, z).wait_send())
    each(4, x, lambda to: x_copy(to, x).wait_send())
    each(8, z, lambda to: z_copy(s3, r4, zz_send, zz_recv, to, z).wait_send())
    each(8, mine, lambda to: a_copy(r4, r5, aa_send, aa_recv, to, mine).wait_send())
    store_vgrad.wait()
    store_feat.wait()
    store_kgrad.wait()


def shards(volume, weights, cotangent):
    dma = pltpu.SemaphoreType.DMA
    outs = (
        jax.ShapeDtypeStruct((CO, 64, 64), BF),
        jax.ShapeDtypeStruct((CI, 4, 64, 128), BF),
        jax.ShapeDtypeStruct((3, 3, 3, CI, CO), F32),
    )
    scratch = [pltpu.VMEM(value.shape, BF) for _, value in CONSTANTS] + [
        pltpu.VMEM((CI, 4, 64, 128), BF),
        pltpu.VMEM((3, 3, 3, CI, CO), BF),
        pltpu.VMEM((CO, 64, 64), BF),
        pltpu.VMEM((CO, 64, 64), BF),
        pltpu.VMEM((CI, 4, 64, 128), BF),
        pltpu.VMEM((3, 3, 3, CI, CO), F32),
        pltpu.VMEM((SLABS + 1, 96, 128), BF),
        pltpu.VMEM((SLABS, 96, 128), BF),
        pltpu.VMEM((SLABS, 96, 128), BF),
        pltpu.VMEM((SLABS + 1, 96, 128), BF),
        pltpu.VMEM((128, 640), F32),
        pltpu.VMEM((QB, 9 * 256), BF),
        pltpu.VMEM((256, 1280), BF),
        pltpu.VMEM((256, 640), BF),
        pltpu.VMEM((512, 640), BF),
        pltpu.VMEM((BANDS, 1536, 256), BF),
        pltpu.VMEM((BANDS + 1, 1280, 256), BF),
        pltpu.VMEM((2, 64, 128), F32),
        pltpu.VMEM((64 * GROUPS, 1024), BF),
        pltpu.VMEM((64 * GROUPS, 1024), BF),
        pltpu.VMEM((8, 8, 8, 128), F32),
        pltpu.VMEM((8, 8, 8, 128), F32),
        pltpu.VMEM((8, 8, 128), F32),
        pltpu.VMEM((8, 8, 128), F32),
        pltpu.VMEM((8, 128), F32),
        pltpu.VMEM((4, 8, 128), F32),
        pltpu.VMEM((8, 128), F32),
        pltpu.VMEM((8, 8, 128), F32),
        pltpu.VMEM((8, 8, 8, 128), F32),
        dma((3,)), dma((NC,)), dma((3,)),
        dma((SLABS,)), dma((SLABS,)), dma((SLABS,)), dma((SLABS,)),
        dma((8,)), dma((8,)), dma((8,)), dma((8,)), dma((4,)), dma((4,)),
        dma((8,)), dma((8,)), dma((8,)), dma((8,)),
    ]
    anywhere = pl.BlockSpec(memory_space=pl.ANY)
    features, volume_grad, kernel_grad = pl.pallas_call(
        kernel,
        out_shape=outs,
        in_specs=[anywhere] * (3 + NC),
        out_specs=(anywhere,) * 3,
        scratch_shapes=scratch,
        compiler_params=pltpu.CompilerParams(
            collective_id=0, has_side_effects=True, vmem_limit_bytes=56 << 20),
        cost_estimate=pl.CostEstimate(
            flops=2 * 10**10, bytes_accessed=8 << 20, transcendentals=0),
    )(
        volume[0],
        jnp.transpose(weights, (2, 3, 4, 1, 0)),
        cotangent[0, :, :, 0, :],
        *[jnp.asarray(value) for _, value in CONSTANTS],
    )
    return (
        features[None, :, :, None, :],
        volume_grad[None],
        jnp.transpose(kernel_grad, (4, 3, 0, 1, 2)),
    )


def solution(mesh):
    placed = (P("vol", None, "gz", None, None), P(), P("vol", None, None, "gz", None))
    return jax.shard_map(
        shards,
        mesh=mesh,
        in_specs=placed,
        out_specs=(P("vol", None, None, "gz", None), P("vol", None, "gz", None, None), P()),
        check_vma=False,
    )
```

time: 529 us -> 71.5 us (0.14)
  waiting for transfers between devices: 239 us -> 0 us
  local copies, waits for them, and re-layouts: 130 us -> 4.5 us
  matrix products: 89.3 us -> 0 us
  Pallas kernels: 0 us -> 66.2 us
  starting transfers between devices: 31.5 us -> 0 us
  other arithmetic: 20.4 us -> 0 us
  between operations: 14.4 us -> 0.65 us
    psum x1 -> x0, waiting for transfers between devices: 239 us -> none  [shards(): summed = lax.psum(partial_grad, ('vol', 'gz'))]
    conv_general_dilated x3 -> x0, matrix products: 89.3 us -> none  [the longest x1 58.6 us: shards(): lax.conv_general_dilated(padded, slab_grad, (1, 1, 1), 'VALID', rhs_dilat...]
    pallas_call x0 -> x1, Pallas kernels: none -> 66.2 us  [shards(): pl.pallas_call(kernel, out_shape=outs, in_specs=[anywhere] * (3 + NC), ou...]
    conv_general_dilated x6 -> x0, local copies, waits for them, and re-layouts: 44.2 us -> none  [the longest x4 26.8 us: transpose_conv(): lax.conv_general_dilated(grads, flipped, (1, 1, 1), ((2, 2), (2, 2), (2,...]
    concatenate x3 -> x0, local copies, waits for them, and re-layouts: 30.5 us -> none  [shards(): jnp.concatenate([under_plane, volume], axis=2)]
    unnamed x20 -> x7, local copies, waits for them, and re-layouts: 29.7 us -> 4.5 us
    all_to_all x2 -> x0, starting transfers between devices: 22.7 us -> none  [the longest x1 13.3 us: shards(): lax.all_to_all(slab_out, 'gz', split_axis=3, concat_axis=2, tiled=True)]
    all_to_all x3 -> x0, local copies, waits for them, and re-layouts: 14.5 us -> none  [the longest x2 13.8 us: shards(): lax.all_to_all(cotangent, 'gz', split_axis=2, concat_axis=3, tiled=True)]
  transfers between devices with their start and end apart: 5 -> 0, of which waited for: 1 -> 0; matrix products, arithmetic and copies ran while one was open for 44% -> 0% of each run, Pallas kernels for 0% -> 0%
where the time goes in v1:
time: 71.5 us; the launch traced here: 71.4 us
  Pallas kernels  66.2 us (93%)
  local copies, waits for them, and re-layouts  4.5 us (6%)
    pallas_call x1, Pallas kernels, shards(): pl.pallas_call(kernel, out_shape=outs, in_specs=[anywhere] * (3 + NC), ou...  66.2 us
    unnamed x7, local copies, waits for them, and re-layouts  4.5 us

profile of v1, /device:TPU:1, one launch (start us, length us, event | category | flops | bytes accessed | tf_op | source)
XLA Modules:
  0.0 71.4 jit_solution(10509167923389730650)
XLA Ops:
  0.6 66.2 %shard_map.175 = (bf16[64,64,64]{2,1,0:T(8,128)(2,1)}, bf16[32,4,64,128]{3,2,1,0:T(8,128)(2,1)}, f32[3,3,3,32,64]{4,3,2,1,0:T(8,128)}) custom-call(bf16[32,4,64,128]{3,2,1,0:T(8,128)(2,1)} %bitcast.11, bf16[3,3,3,32,64]{4,3,2,1,0:T(8,128)(2,1)} %bitcast.13, bf16[64,64,64]{2,1,0:T(8,128)(2,1)} %bitcast.12, bf16[64,256]{1,0:T(8,128)(2,1)} %constant.26.clone.refs_3_, ...), custom_call_target="tpu_custom_call" | custom-call | flops 20000000000 | bytes 8388608 | tf_op jit(solution)/shard_map/pallas_call | solution.py:502
  66.9 0.0 copy-start
  66.9 2.4 %copy.23 = bf16[1,64,64,1,64]{4,2,3,1,0:T(8,128)(2,1)} copy(bf16[1,64,64,1,64]{4,2,3,1,0:T(8,128)(2,1)} %bitcast.9) | data formatting | bytes 1048576
  69.3 0.0 copy-done
  69.3 0.0 copy-start.1
  69.3 1.3 %copy.24 = bf16[1,32,4,64,128]{4,3,2,1,0:T(8,128)(2,1)} copy(bf16[1,32,4,64,128]{4,3,2,1,0:T(8,128)(2,1)S(1)} %bitcast.8) | data formatting | bytes 4194304
  70.6 0.0 copy-done.1
  70.6 0.8 %copy.25 = f32[64,32,3,3,3]{0,1,4,3,2:T(8,128)} copy(f32[64,32,3,3,3]{0,1,4,3,2:T(8,128)S(1)} %bitcast.10) | data formatting | bytes 442368
Async XLA Ops:
  66.9 2.4 %copy-start = (bf16[32,4,64,128]{3,2,1,0:T(8,128)(2,1)S(1)}, bf16[32,4,64,128]{3,2,1,0:T(8,128)(2,1)}, u32[]{:S(2)}) copy-start(bf16[32,4,64,128]{3,2,1,0:T(8,128)(2,1)} %get-tuple-element.7) | copy-start | bytes 6291460
  69.3 1.3 %copy-start.1 = (f32[3,3,3,32,64]{4,3,2,1,0:T(8,128)S(1)}, f32[3,3,3,32,64]{4,3,2,1,0:T(8,128)}, u32[]{:S(2)}) copy-start(f32[3,3,3,32,64]{4,3,2,1,0:T(8,128)} %get-tuple-element.8) | copy-start | bytes 663556

commit v2 on v1

v2 whole, which is shorter than its diff:
```python
import functools

import jax
import jax.numpy as jnp
import numpy as np
from jax import lax
from jax.experimental import pallas as pl
from jax.experimental.pallas import tpu as pltpu
from jax.sharding import PartitionSpec as P

MESH = pl.DeviceIdType.MESH
BF = jnp.bfloat16
F32 = jnp.float32

CI, CO, SLABS, BANDS = 32, 64, 32, 4
QB = 5 * CO

BACK = ((0, 0), (0, 2), (2, 2), (2, 0), (0, 1), (2, 1), (1, 2), (1, 0), (1, 1))
FRONT = ((1, 0), (1, 1), (1, 2), (2, 0), (2, 1), (2, 2), (0, 0), (0, 1), (0, 2))
TAPS = tuple((a, b, e) for e in range(3) for a in (1, 2, 0) for b in range(3))
GROUPS = 7


def one_hot(rows, columns, test):
    row, column = np.meshgrid(np.arange(rows), np.arange(columns), indexing="ij")
    return np.asarray(test(row, column), np.float32).astype(jnp.bfloat16)


def pair_pick(row, column):
    half, o, p = column // 256, column // 16 % 16, column % 16
    return (row % 16 == o) & (p == 2 * (row // 16) + half)


def even_pick(row, column):
    o, p = column // 16 % 16, column % 16
    return (row % 16 == o) & (p == 2 * (row // 16))


def unpick(row, column):
    half, slab, o = column // 128, column // 16 % 8, column % 16
    return (row // 16 == o) & (row % 16 == 2 * slab + half)


def place(row, column):
    ql, c, yl = row // 256, row // 8 % 32, row % 8
    b, channel = column // 32, column % 32
    return (b < 3) & (c == channel) & (yl == 2 * ql + b - 1)


def spread_x(row, column):
    zz, x = row // 128, row % 128
    e, half, r = column // 128, column // 64 % 2, column % 64
    return (zz == half) & (x == 2 * r + e - 1)


def weave_x(row, column):
    parity, zz, r = row // 128, row // 64 % 2, row % 64
    return (zz == column // 128) & (column % 128 == 2 * r + parity)


def shift_left(row, column):
    return (column % 64 < 63) & (row == column + 1)


def later_planes(high, row, column):
    shift = 1 - column // 128
    lane = column % 128 + shift
    valid = (column % 64 + shift) < 64
    return valid & (row == np.where(lane < 64, lane + 64, 128 + lane - (0 if high else 64)))


def squeeze(row, column):
    return (row // 128 == column // 64) & (row % 128 == column % 64)


def halves(row, column):
    return (column % 64 == row) & ((column // 64 == 0) | (column // 64 == 3))


def join(upper, row, column):
    even = (row == column) | (row == 128 + 64 * upper + column)
    odd = row == column - 64
    return np.where(column < 64, even, (column // 64 == 2) & odd)


def sum_band(row, column):
    return row // 8 == column


CONSTANTS = (
    ("halves", one_hot(64, 256, halves)),
    ("pairs", one_hot(128, 512, pair_pick)),
    ("evens", one_hot(128, 512, even_pick)),
    ("place", one_hot(5 * 256, 128, place)),
    ("place_t", np.ascontiguousarray(one_hot(5 * 256, 128, place).T)),
    ("spread", one_hot(256, 384, spread_x)),
    ("squeeze", one_hot(256, 128, squeeze)),
    ("shift", one_hot(128, 128, shift_left)),
    ("later_lo", one_hot(256, 256, functools.partial(later_planes, False))),
    ("later_hi", one_hot(256, 256, functools.partial(later_planes, True))),
    ("bands", one_hot(1024, 128, sum_band)),
    ("weave", one_hot(256, 256, weave_x)),
    ("join_lo", one_hot(256, 256, functools.partial(join, 0))),
    ("join_hi", one_hot(256, 256, functools.partial(join, 1))),
    ("unpick", one_hot(256, 256, unpick)),
)
NC = len(CONSTANTS)


def dot(a, b):
    return jnp.dot(a, b, preferred_element_type=F32)


def dot_nt(a, b):
    return lax.dot_general(a, b, (((1,), (1,)), ((), ())), preferred_element_type=F32)


def kernel(*refs):
    (vol_in, w_in, cot_in), refs = refs[:3], refs[3:]
    const_in, refs = refs[:NC], refs[NC:]
    (feat, vgrad, gathered), refs = refs[:3], refs[3:]
    const, refs = refs[:NC], refs[NC:]
    k = {name: ref for (name, _), ref in zip(CONSTANTS, const)}
    (vol, w, cot, cs, cr, near, fw, late_in, fs, rf, wa, tc, tt_oo, tt_oe, tt_e, vc, c4, carry,
     dh, dl, terms, part_in, part, whole_in, whole,
     in_sem, const_sem, cot_send, cot_recv, near_send, near_recv, late_send, late_recv,
     ft_send, ft_recv, part_send, part_recv, whole_send, whole_recv, last_send, last_recv) = refs

    mv, mg = lax.axis_index("vol"), lax.axis_index("gz")
    y, z_lo = mv % 4, mv // 4
    core, z_hi, x = mg % 2, mg // 2 % 4, mg // 8
    mine, z = x * 8 + y * 2 + core, z_hi * 2 + z_lo

    barrier = pltpu.get_barrier_semaphore()

    def greet(v, g):
        pl.semaphore_signal(barrier, inc=1, device_id=(v, g), device_id_type=MESH)

    def greet_slab(i, _):
        greet(mv, (mg + i) % SLABS)
        return 0

    lax.fori_loop(1, SLABS, greet_slab, 0)

    def greet_layer(i, _):
        greet(z_lo * 4 + (y + i // 8) % 4, (i % 8 // 2) * 8 + z_hi * 2 + i % 2)
        return 0

    lax.fori_loop(8, 32, greet_layer, 0)
    for other in range(4):
        greet((1 - z_lo) * 4 + y, x * 8 + other * 2 + core)

    load_cot = pltpu.make_async_copy(cot_in, cot, in_sem.at[0])
    load_w = pltpu.make_async_copy(w_in, w, in_sem.at[1])
    load_vol = pltpu.make_async_copy(vol_in, vol, in_sem.at[2])
    loads = {
        name: pltpu.make_async_copy(const_in[i], const[i], const_sem.at[i])
        for i, (name, _) in enumerate(CONSTANTS)
    }
    load_cot.start()
    for name in ("halves", "pairs", "evens"):
        loads[name].start()
    load_w.start()
    load_vol.start()
    for name in list(loads)[3:]:
        loads[name].start()

    cs[SLABS, 64:96, :] = jnp.zeros((32, 128), BF)
    rf[0, 64:96, :] = jnp.zeros((32, 128), BF)
    for slot in range(1, SLABS, 2):
        rf[slot, 64:96, :] = jnp.zeros((32, 128), BF)
    c4[BANDS, 1024:1280, 128:256] = jnp.zeros((256, 128), BF)
    dh[384:448, 768:1024] = jnp.zeros((64, 256), BF)
    dl[384:448, 768:1024] = jnp.zeros((64, 256), BF)
    terms[28:32] = jnp.zeros((4, 16, 128), F32)
    carry[...] = jnp.zeros((2, 64, 128), F32)

    load_cot.wait()
    for name in ("halves", "pairs", "evens"):
        loads[name].wait()

    def pack(m, _):
        wide = []
        for g in range(4):
            block = cot[16 * g : 16 * g + 16, pl.ds(16 * m, 16), :].reshape(256, 64)
            wide.append(dot(block, k["halves"][...]).astype(BF))
        for g in range(4):
            both = jnp.concatenate([wide[g][:, :128], wide[g][:, 128:]], axis=0)
            two = dot(k["pairs"][...], both).astype(BF)
            cs[pl.ds(8 * m + 1, 8), 16 * g : 16 * g + 16, :] = two.reshape(8, 16, 128)
        for g in range(2):
            both = jnp.concatenate([wide[g][:, :128], wide[g + 2][:, 128:]], axis=0)
            two = dot(k["evens"][...], both).astype(BF)
            cs[pl.ds(8 * m, 8), 64 + 16 * g : 80 + 16 * g, :] = two.reshape(8, 16, 128)
        return 0

    lax.fori_loop(0, 4, pack, 0)

    pl.semaphore_wait(barrier, 59)

    def cot_copy(to, rows):
        return pltpu.make_async_remote_copy(
            src_ref=cs.at[to + 1, 0:rows], dst_ref=cr.at[mg, 0:rows],
            send_sem=cot_send.at[0], recv_sem=cot_recv.at[0],
            device_id=(mv, to), device_id_type=MESH)

    cr[mg, 0:64] = cs[mg + 1, 0:64]

    @pl.when(core == 1)
    def _():
        cr[mg, 64:96] = cs[mg + 1, 64:96]

    def send_cot(i, _):
        to = (mg + i) % SLABS

        @pl.when(to % 2 == 0)
        def _():
            cot_copy(to, 64).start()

        @pl.when(to % 2 == 1)
        def _():
            cot_copy(to, 96).start()

        return 0

    lax.fori_loop(1, SLABS, send_cot, 0)

    def arrived(buffer, sem):
        pltpu.make_async_copy(buffer, buffer, sem.at[0]).wait()

    load_w.wait()
    wa[...] = jnp.zeros((128, 640), F32)
    for b in range(3):
        for i in range(0, 10, 2):
            (a, e), rows = BACK[i], slice(32 * b, 32 * b + 32)
            first = w[a, b, e].astype(F32)
            if i + 1 < 9:
                a, e = BACK[i + 1]
                second = w[a, b, e].astype(F32)
            else:
                second = jnp.zeros((32, 64), F32)
            wa[rows, 64 * i : 64 * i + 128] = jnp.concatenate([first, second], axis=1)
    for name in ("place", "place_t"):
        loads[name].wait()
    taps = wa[...]
    back = taps.astype(BF)
    front = jnp.transpose(taps).astype(BF)
    for ql in range(5):
        t = dot(k["place"][256 * ql : 256 * ql + 256, :], back).astype(BF)
        tt_oo[:, 256 * ql : 256 * ql + 256] = t[:, 0:256]
        tt_oe[:, 128 * ql : 128 * ql + 128] = t[:, 256:384]
        tt_e[0:256, 128 * ql : 128 * ql + 128] = t[:, 384:512]
        tt_e[256:512, 128 * ql : 128 * ql + 128] = t[:, 512:640]
        t = dot(front, k["place_t"][:, 256 * ql : 256 * ql + 256]).astype(BF)
        for i, pair in enumerate(FRONT):
            j = BACK.index(pair)
            tc[64 * ql : 64 * ql + 64, 256 * i : 256 * i + 256] = t[64 * j : 64 * j + 64, :]

    load_vol.wait()
    loads["spread"].wait()

    def split_x(n, _):
        for parity in range(2):
            both = jnp.concatenate(
                [vol[:, 2 * zz + parity, pl.ds(16 * n, 16), :].reshape(512, 128) for zz in range(2)],
                axis=1)
            s = dot(both, k["spread"][...]).reshape(CI, 16, 384)
            for h in range(2):
                part = s[:, 8 * h : 8 * h + 8, :].reshape(256, 384).astype(BF)
                for e in range(3):
                    row = (3 * parity + e) * 256
                    vc[n, row : row + 256, 128 * h : 128 * h + 128] = part[:, 128 * e : 128 * e + 128]
        return 0

    lax.fori_loop(0, BANDS, split_x, 0)

    lane = lax.broadcasted_iota(jnp.int32, (256, 128), 1)

    def ft_copy(to, rows):
        return pltpu.make_async_remote_copy(
            src_ref=fs.at[to, 0:rows], dst_ref=rf.at[mg + 1, 0:rows],
            send_sem=ft_send.at[0], recv_sem=ft_recv.at[0],
            device_id=(mv, to), device_id_type=MESH)

    def forward(n, _):
        f01 = dot(tc[:, :1536], vc[n])
        f12 = dot(tc[:, 1536:], vc[n, 768:1536, :])
        for h in range(2):
            a, b = f01[:, 128 * h : 128 * h + 128], f12[:, 128 * h : 128 * h + 128]
            own = jnp.concatenate([a[0:64] + carry[0], a[64:256]], axis=0)
            late = jnp.concatenate([b[0:64] + carry[1], b[64:256]], axis=0)
            carry[0], carry[1] = a[256:320], b[256:320]
            swapped = pltpu.roll(late, 64, 1)
            total = own + jnp.where(lane >= 64, swapped, 0.0)
            for ql in range(4):
                q = 8 * n + 4 * h + ql
                low, high = swapped[64 * ql : 64 * ql + 32], late[64 * ql + 32 : 64 * ql + 64]
                fw[q] = total[64 * ql : 64 * ql + 64]
                fs[q, 64:96, :] = jnp.where(lane[0:32] < 64, low, high).astype(BF)
        return 0

    lax.fori_loop(0, BANDS, forward, 0)

    late_copy = pltpu.make_async_remote_copy(
        src_ref=fs.at[:, 64:96], dst_ref=late_in, send_sem=late_send.at[0], recv_sem=late_recv.at[0],
        device_id=(mv, mg + 1 - 2 * core), device_id_type=MESH)

    @pl.when(core == 0)
    def _():
        late_copy.start()

        def round_off(q, _):
            fs[q, 0:64] = fw[q].astype(BF)
            return 0

        lax.fori_loop(0, SLABS, round_off, 0)
        rf[mg + 1, 0:64] = fs[mg, 0:64]

    @pl.when(core == 1)
    def _():
        late_copy.wait_recv()

        def add_late(q, _):
            both = late_in[q].astype(F32)
            both = jnp.concatenate([both, pltpu.roll(both, 64, 1)], axis=0)
            fs[q, 0:64] = (fw[q] + jnp.where(lane[0:64] < 64, both, 0.0)).astype(BF)
            return 0

        lax.fori_loop(0, SLABS, add_late, 0)
        rf[mg + 1] = fs[mg]

    def send_ft(i, _):
        to = (mg + i) % SLABS

        @pl.when(core == 0)
        def _():
            ft_copy(to, 64).start()

        @pl.when(core == 1)
        def _():
            ft_copy(to, 96).start()

        return 0

    @pl.when(core == 0)
    def _():
        arrived(cr.at[0:31, 0:64], cot_recv)

    @pl.when(core == 1)
    def _():
        arrived(cr.at[0:31, 0:96], cot_recv)

    near_copy = pltpu.make_async_remote_copy(
        src_ref=near, dst_ref=cr.at[:, 64:96], send_sem=near_send.at[0], recv_sem=near_recv.at[0],
        device_id=(mv, mg + 1 - 2 * core), device_id_type=MESH)
    for name in ("squeeze", "shift", "later_lo", "later_hi"):
        loads[name].wait()

    @pl.when(core == 1)
    def _():
        def pass_on(n, _):
            rows = jnp.concatenate(
                [jnp.concatenate([cr[8 * n + i, 0:32], cr[8 * n + i, 32:64]], axis=1) for i in range(8)],
                axis=0)
            near[pl.ds(8 * n, 8)] = dot(rows, k["squeeze"][...]).astype(BF).reshape(8, 32, 128)
            return 0

        lax.fori_loop(0, BANDS, pass_on, 0)
        near_copy.start()

    lax.fori_loop(1, SLABS, send_ft, 0)

    def keep(n, h, ql, row, value):
        size = value.shape[0]
        c4[n + 1, 256 * ql + row : 256 * ql + row + size, 128 * h : 128 * h + 128] = value
        if ql == 0:
            c4[n + h, 1024 + row : 1024 + row + size, 128 * (1 - h) : 128 * (2 - h)] = value

    def forms_own(n, _):
        blocks = [cr[8 * n + i, 0:64] for i in range(8)]
        moved = dot(jnp.concatenate(blocks, axis=0), k["shift"][...]).astype(BF)
        for i in range(8):
            keep(n, i // 4, i % 4, 128, blocks[i])
            keep(n, i // 4, i % 4, 192, moved[64 * i : 64 * i + 64])
        return 0

    lax.fori_loop(0, BANDS, forms_own, 0)

    def forms_later(n, _):
        blocks = [cr[8 * n + i] for i in range(8)]
        for part_, name in ((0, "later_lo"), (1, "later_hi")):
            rows = jnp.concatenate(
                [jnp.concatenate([v[32 * part_ : 32 * part_ + 32], v[64:96]], axis=1) for v in blocks],
                axis=0)
            made = dot(rows, k[name][...]).astype(BF)
            for i in range(8):
                new = made[32 * i : 32 * i + 32]
                keep(n, i // 4, i % 4, 32 * part_, new[:, 0:128])
                keep(n, i // 4, i % 4, 64 + 32 * part_, new[:, 128:256])
        return 0

    yl = lax.broadcasted_iota(jnp.int32, (64, 256), 1) % 8

    def gradient(i, e):
        total = None
        start, taps = (64 if i == 2 else 128), 256 * (e + (0 if i == 0 else 3))
        for n in range(BANDS):
            rows = jnp.concatenate(
                [c4[n + 1, 256 * ql + start : 256 * ql + start + 64, :] for ql in range(5)], axis=0)
            term = dot_nt(rows, vc[n, taps : taps + 256, :])
            total = term if total is None else total + term
        g = [total[64 * ql : 64 * ql + 64] for ql in range(5)]
        d0 = jnp.where(yl == 1, g[1], jnp.where(yl == 3, g[2], jnp.where(
            yl == 5, g[3], jnp.where(yl == 7, g[4], 0.0))))
        rest = jnp.where(yl < 2, g[0], jnp.where(yl < 4, g[1], jnp.where(yl < 6, g[2], g[3])))
        d1, d2 = jnp.where(yl % 2 == 0, rest, 0.0), jnp.where(yl % 2 == 1, rest, 0.0)
        for b, d in enumerate((d0, d1, d2)):
            group, slot = divmod(9 * e + 3 * i + b, 4)
            at = (slice(64 * group, 64 * group + 64), slice(256 * slot, 256 * slot + 256))
            top = d.astype(BF)
            dh[at] = top
            dl[at] = (d - top.astype(F32)).astype(BF)

    for e in range(3):
        gradient(0, e)
        gradient(1, e)

    @pl.when(core == 0)
    def _():
        near_copy.wait_recv()

    lax.fori_loop(0, BANDS, forms_later, 0)
    for e in range(3):
        gradient(2, e)
    loads["bands"].wait()
    packed = dot(dh[...], k["bands"][...]) + dot(dl[...], k["bands"][...])
    terms[0:28] = packed.reshape(28, 16, 128)

    def layer_copy(source, target, send, recv, to, slot):
        return pltpu.make_async_remote_copy(
            src_ref=source, dst_ref=target.at[slot], send_sem=send.at[0], recv_sem=recv.at[0],
            device_id=(z_lo * 4 + to // 2 % 4, to // 8 * 8 + z_hi * 2 + to % 2), device_id_type=MESH)

    def part_copy(to, slot):
        return layer_copy(terms.at[to], part_in, part_send, part_recv, to, slot)

    def last_copy(to, slot):
        return layer_copy(whole, gathered, last_send, last_recv, to, slot)

    def whole_copy(to, slot):
        return pltpu.make_async_remote_copy(
            src_ref=part, dst_ref=whole_in.at[slot],
            send_sem=whole_send.at[0], recv_sem=whole_recv.at[0],
            device_id=(to % 2 * 4 + y, x * 8 + to // 2 * 2 + core), device_id_type=MESH)

    loads["weave"].wait()

    def backward(n):
        c = [c4[n + 1, 256 * ql : 256 * ql + 256, :] for ql in range(5)]
        oo = dot(tt_oo[...], c4[n + 1])
        oe = dot(tt_oe[...], jnp.concatenate([v[64:192] for v in c], axis=0))
        ev = dot(tt_e[...], jnp.concatenate([v[128:256] for v in c], axis=0))
        for parity, (at_even, at_odd) in enumerate(((ev[256:512], ev[0:256]), (oe, oo))):
            even, odd = at_even.astype(BF), at_odd.astype(BF)
            parts = []
            for h in range(2):
                lanes = slice(128 * h, 128 * h + 128)
                both = jnp.concatenate([even[:, lanes], odd[:, lanes]], axis=1)
                parts.append(dot(both, k["weave"][...]).reshape(CI, 8, 256))
            out = jnp.concatenate(parts, axis=1).astype(BF)
            for zz in range(2):
                vgrad[:, 2 * zz + parity, 16 * n : 16 * n + 16, :] = out[:, :, 128 * zz : 128 * zz + 128]

    def each(count, me, act):
        def step(i, _):
            act((me + i) % count)
            return 0

        lax.fori_loop(1, count, step, 0)

    each(32, mine, lambda to: part_copy(to, mine).start())
    part_in[mine] = terms[mine]

    @pl.when(core == 0)
    def _():
        late_copy.wait_send()
        arrived(vc.at[0, 0:1248], cot_send)

    @pl.when(core == 1)
    def _():
        near_copy.wait_send()
        arrived(vc.at[0, 0:1232], cot_send)

    backward(0)
    arrived(part_in.at[0:31], part_recv)
    part[...] = functools.reduce(jnp.add, [part_in[i] for i in range(32)])

    each(8, z, lambda to: whole_copy(to, z).start())
    whole_in[z] = part[...]
    arrived(terms.at[0:31], part_send)
    backward(1)
    arrived(whole_in.at[0:7], whole_recv)
    whole[...] = (functools.reduce(jnp.add, [whole_in[i] for i in range(8)]) * 0.125).astype(BF)

    each(32, mine, lambda to: last_copy(to, mine).start())
    gathered[mine] = whole[...]
    arrived(whole_in.at[0:7], whole_send)
    backward(2)
    backward(3)

    @pl.when(core == 0)
    def _():
        arrived(vc.at[0, 0:1248], ft_recv)
        arrived(fs.at[0:31, 0:64], ft_send)

    @pl.when(core == 1)
    def _():
        arrived(vc.at[0, 0:1232], ft_recv)
        arrived(fs.at[0:31, 0:96], ft_send)

    for name in ("join_lo", "join_hi", "unpick"):
        loads[name].wait()

    def unpack(m, _):
        for g in range(4):
            two = rf[pl.ds(8 * m + 1, 8), 16 * g : 16 * g + 16, :].reshape(128, 128)
            row = 64 + 16 * (g % 2)
            one = rf[pl.ds(8 * m, 8), row : row + 16, :].reshape(128, 128)
            summed = k["join_hi"] if g >= 2 else k["join_lo"]
            planes = dot(jnp.concatenate([two, one], axis=1), summed[...]).astype(BF)
            planes = jnp.concatenate([planes[:, 0:128], planes[:, 128:256]], axis=0)
            rows = dot(k["unpick"][...], planes)[:, 0:64].astype(BF)
            feat[16 * g : 16 * g + 16, pl.ds(16 * m, 16), :] = rows.reshape(16, 16, 64)
        return 0

    lax.fori_loop(0, 4, unpack, 0)

    arrived(gathered.at[0:31], last_recv)
    arrived(gathered.at[0:31], last_send)


def store(feat, vgrad, gathered, feat_out, vgrad_out, kgrad_out, kgrad, sem):
    copies = [
        pltpu.make_async_copy(source, target, sem.at[i])
        for i, (source, target) in enumerate(
            ((vgrad, vgrad_out), (feat, feat_out), (kgrad, kgrad_out)))
    ]
    copies[0].start()
    copies[1].start()
    for g in range(GROUPS):
        total = jnp.transpose(gathered[4 * g : 4 * g + 4].astype(F32).reshape(64, 128))
        for slot in range(4):
            if 4 * g + slot < len(TAPS):
                kgrad[TAPS[4 * g + slot]] = total[32 * slot : 32 * slot + 32]
    copies[2].start()
    for copy in copies:
        copy.wait()


def shards(volume, weights, cotangent):
    dma = pltpu.SemaphoreType.DMA
    outs = (
        jax.ShapeDtypeStruct((CO, 64, 64), BF),
        jax.ShapeDtypeStruct((CI, 4, 64, 128), BF),
        jax.ShapeDtypeStruct((3, 3, 3, CI, CO), F32),
    )
    held = (
        pltpu.VMEM((CO, 64, 64), BF),
        pltpu.VMEM((CI, 4, 64, 128), BF),
        pltpu.VMEM((32, 16, 128), BF),
    )
    scratch = [pltpu.VMEM(value.shape, BF) for _, value in CONSTANTS] + [
        pltpu.VMEM((CI, 4, 64, 128), BF),
        pltpu.VMEM((3, 3, 3, CI, CO), BF),
        pltpu.VMEM((CO, 64, 64), BF),
        pltpu.VMEM((SLABS + 1, 96, 128), BF),
        pltpu.VMEM((SLABS, 96, 128), BF),
        pltpu.VMEM((SLABS, 32, 128), BF),
        pltpu.VMEM((SLABS, 64, 128), F32),
        pltpu.VMEM((SLABS, 32, 128), BF),
        pltpu.VMEM((SLABS, 96, 128), BF),
        pltpu.VMEM((SLABS + 1, 96, 128), BF),
        pltpu.VMEM((128, 640), F32),
        pltpu.VMEM((QB, 9 * 256), BF),
        pltpu.VMEM((256, 1280), BF),
        pltpu.VMEM((256, 640), BF),
        pltpu.VMEM((512, 640), BF),
        pltpu.VMEM((BANDS, 1536, 256), BF),
        pltpu.VMEM((BANDS + 1, 1280, 256), BF),
        pltpu.VMEM((2, 64, 128), F32),
        pltpu.VMEM((64 * GROUPS, 1024), BF),
        pltpu.VMEM((64 * GROUPS, 1024), BF),
        pltpu.VMEM((32, 16, 128), F32),
        pltpu.VMEM((32, 16, 128), F32),
        pltpu.VMEM((16, 128), F32),
        pltpu.VMEM((8, 16, 128), F32),
        pltpu.VMEM((16, 128), BF),
        dma((3,)), dma((NC,)),
        *[dma((1,))] * 14,
    ]
    anywhere = pl.BlockSpec(memory_space=pltpu.HBM)
    inside = pl.BlockSpec(memory_space=pltpu.VMEM)
    results = pl.pallas_call(
        kernel,
        out_shape=held,
        in_specs=[anywhere] * (3 + NC),
        out_specs=(inside,) * 3,
        scratch_shapes=scratch,
        compiler_params=pltpu.CompilerParams(
            collective_id=0, has_side_effects=True, vmem_limit_bytes=40 << 20),
        cost_estimate=pl.CostEstimate(
            flops=2 * 10**10, bytes_accessed=8 << 20, transcendentals=0),
    )(*[
        pltpu.with_memory_space_constraint(value, pltpu.HBM)
        for value in (
            volume[0],
            jnp.transpose(weights, (2, 3, 4, 1, 0)),
            cotangent[0, :, :, 0, :],
            *[jnp.asarray(value) for _, value in CONSTANTS],
        )
    ])
    features, volume_grad, kernel_grad = pl.pallas_call(
        store,
        out_shape=outs,
        in_specs=[inside] * 3,
        out_specs=(anywhere,) * 3,
        scratch_shapes=[pltpu.VMEM((3, 3, 3, CI, CO), F32), dma((3,))],
        compiler_params=pltpu.CompilerParams(vmem_limit_bytes=8 << 20),
    )(*[pltpu.with_memory_space_constraint(value, pltpu.VMEM) for value in results])
    return (
        features[None, :, :, None, :],
        volume_grad[None],
        jnp.transpose(kernel_grad, (4, 3, 0, 1, 2)),
    )


def solution(mesh):
    placed = (P("vol", None, "gz", None, None), P(), P("vol", None, None, "gz", None))
    return jax.shard_map(
        shards,
        mesh=mesh,
        in_specs=placed,
        out_specs=(P("vol", None, None, "gz", None), P("vol", None, "gz", None, None), P()),
        check_vma=False,
    )
```

time: 71.5 us -> 57.9 us (0.81)
  Pallas kernels: 66.2 us -> 57.2 us
  local copies, waits for them, and re-layouts: 4.5 us -> 0 us
    pallas_call x1 -> x2, Pallas kernels: 66.2 us -> 57.2 us  [the longest x1 55.4 us: shards(): pl.pallas_call(kernel, out_shape=held, in_specs=[anywhere] * (3 + NC), ou...]
    unnamed x7 -> x0, local copies, waits for them, and re-layouts: 4.5 us -> none
where the time goes in v2:
time: 57.9 us
  Pallas kernels  57.2 us (99%)
  between operations  0.64 us (1%)
    pallas_call x1, Pallas kernels, shards(): pl.pallas_call(kernel, out_shape=held, in_specs=[anywhere] * (3 + NC), ou...  55.4 us
    pallas_call x1, Pallas kernels, shards(): pl.pallas_call(store, out_shape=outs, in_specs=[inside] * 3, out_specs=(a...  1.83 us

profile of v2, /device:TPU:1, one launch (start us, length us, event | category | flops | bytes accessed | tf_op | source)
XLA Modules:
  0.0 57.9 jit_solution(10486451918485825276)
XLA Ops:
  0.6 55.4 %shard_map.193 = (bf16[64,64,64]{2,1,0:T(8,128)(2,1)S(1)}, bf16[32,4,64,128]{3,2,1,0:T(8,128)(2,1)S(1)}, bf16[32,16,128]{2,1,0:T(8,128)(2,1)S(1)}) custom-call(bf16[32,4,64,128]{3,2,1,0:T(8,128)(2,1)} %bitcast.8, bf16[3,3,3,32,64]{4,3,2,1,0:T(8,128)(2,1)} %bitcast.13, bf16[64,64,64]{2,1,0:T(8,128)(2,1)} %bitcast.10, bf16[64,256]{1,0:T(8,128)(2,1)} %constant.30.clone.refs_3_, ...), custom_call_target="tpu_custom_call" | custom-call | flops 20000000000 | bytes 8388608 | tf_op jit(solution)/shard_map/pallas_call | solution.py:603
  56.0 1.8 %shard_map.194 = (bf16[64,64,64]{2,1,0:T(8,128)(2,1)}, bf16[32,4,64,128]{3,2,1,0:T(8,128)(2,1)}, f32[3,3,3,32,64]{4,3,2,1,0:T(8,128)}) custom-call(bf16[64,64,64]{2,1,0:T(8,128)(2,1)S(1)} %get-tuple-element.9.feat, bf16[32,4,64,128]{3,2,1,0:T(8,128)(2,1)S(1)} %get-tuple-element.10.vgrad, bf16[32,16,128]{2,1,0:T(8,128)(2,1)S(1)} %get-tuple-element.11.gathered), custom_call_target="tpu_custom_call" | custom-call | tf_op jit(solution)/shard_map/pallas_call | solution.py:622

commit v3 on v2

--- a/solution.py
+++ b/solution.py
@@ -211,7 +211,7 @@
         cr[mg, 64:96] = cs[mg + 1, 64:96]
 
     def send_cot(i, _):
-        to = (mg + i) % SLABS
+        to = (mg + 5 * i) % SLABS
 
         @pl.when(to % 2 == 0)
         def _():
@@ -330,7 +330,7 @@
         rf[mg + 1] = fs[mg]
 
     def send_ft(i, _):
-        to = (mg + i) % SLABS
+        to = (mg + 5 * i) % SLABS
 
         @pl.when(core == 0)
         def _():

time: 57.9 us -> 57.6 us (level)
  no operation moved by 1% of the time
where the time goes in v3:
time: 57.6 us; the launch traced here: 57.5 us
  Pallas kernels  56.9 us (99%)
  between operations  0.64 us (1%)
    pallas_call x1, Pallas kernels, shards(): pl.pallas_call(kernel, out_shape=held, in_specs=[anywhere] * (3 + NC), ou...  55 us
    pallas_call x1, Pallas kernels, shards(): pl.pallas_call(store, out_shape=outs, in_specs=[inside] * 3, out_specs=(a...  1.83 us

profile of v3, /device:TPU:1, one launch (start us, length us, event | category | flops | bytes accessed | tf_op | source)
XLA Modules:
  0.0 57.5 jit_solution(18377790976302476265)
XLA Ops:
  0.6 55.0 %shard_map.193 = (bf16[64,64,64]{2,1,0:T(8,128)(2,1)S(1)}, bf16[32,4,64,128]{3,2,1,0:T(8,128)(2,1)S(1)}, bf16[32,16,128]{2,1,0:T(8,128)(2,1)S(1)}) custom-call(bf16[32,4,64,128]{3,2,1,0:T(8,128)(2,1)} %bitcast.8, bf16[3,3,3,32,64]{4,3,2,1,0:T(8,128)(2,1)} %bitcast.13, bf16[64,64,64]{2,1,0:T(8,128)(2,1)} %bitcast.10, bf16[64,256]{1,0:T(8,128)(2,1)} %constant.30.clone.refs_3_, ...), custom_call_target="tpu_custom_call" | custom-call | flops 20000000000 | bytes 8388608 | tf_op jit(solution)/shard_map/pallas_call | solution.py:603
  55.7 1.8 %shard_map.194 = (bf16[64,64,64]{2,1,0:T(8,128)(2,1)}, bf16[32,4,64,128]{3,2,1,0:T(8,128)(2,1)}, f32[3,3,3,32,64]{4,3,2,1,0:T(8,128)}) custom-call(bf16[64,64,64]{2,1,0:T(8,128)(2,1)S(1)} %get-tuple-element.9.feat, bf16[32,4,64,128]{3,2,1,0:T(8,128)(2,1)S(1)} %get-tuple-element.10.vgrad, bf16[32,16,128]{2,1,0:T(8,128)(2,1)S(1)} %get-tuple-element.11.gathered), custom_call_target="tpu_custom_call" | custom-call | tf_op jit(solution)/shard_map/pallas_call | solution.py:622

commit v4 on v3

--- a/solution.py
+++ b/solution.py
@@ -17,8 +17,11 @@
 
 BACK = ((0, 0), (0, 2), (2, 2), (2, 0), (0, 1), (2, 1), (1, 2), (1, 0), (1, 1))
 FRONT = ((1, 0), (1, 1), (1, 2), (2, 0), (2, 1), (2, 2), (0, 0), (0, 1), (0, 2))
-TAPS = tuple((a, b, e) for e in range(3) for a in (1, 2, 0) for b in range(3))
-GROUPS = 7
+TAPS = (
+    *((a, b, e) for e in range(3) for a in (1, 2) for b in range(3)), None, None,
+    *((0, b, e) for e in range(3) for b in range(3)), None, None, None,
+)
+GROUPS, FIRST = 8, 20
 
 
 def one_hot(rows, columns, test):
@@ -170,9 +173,9 @@
     for slot in range(1, SLABS, 2):
         rf[slot, 64:96, :] = jnp.zeros((32, 128), BF)
     c4[BANDS, 1024:1280, 128:256] = jnp.zeros((256, 128), BF)
-    dh[384:448, 768:1024] = jnp.zeros((64, 256), BF)
-    dl[384:448, 768:1024] = jnp.zeros((64, 256), BF)
-    terms[28:32] = jnp.zeros((4, 16, 128), F32)
+    for split in (dh, dl):
+        split[256:320, 512:1024] = jnp.zeros((64, 512), BF)
+        split[448:512, 256:1024] = jnp.zeros((64, 768), BF)
     carry[...] = jnp.zeros((2, 64, 128), F32)
 
     load_cot.wait()
@@ -399,6 +402,30 @@
                 keep(n, i // 4, i % 4, 64 + 32 * part_, new[:, 128:256])
         return 0
 
+    def layer_copy(source, target, send, recv, to, slot):
+        return pltpu.make_async_remote_copy(
+            src_ref=source, dst_ref=target.at[slot], send_sem=send.at[0], recv_sem=recv.at[0],
+            device_id=(z_lo * 4 + to // 2 % 4, to // 8 * 8 + z_hi * 2 + to % 2), device_id_type=MESH)
+
+    def part_copy(to, slot):
+        return layer_copy(terms.at[to], part_in, part_send, part_recv, to, slot)
+
+    def last_copy(to, slot):
+        return layer_copy(whole, gathered, last_send, last_recv, to, slot)
+
+    def whole_copy(to, slot):
+        return pltpu.make_async_remote_copy(
+            src_ref=part, dst_ref=whole_in.at[slot],
+            send_sem=whole_send.at[0], recv_sem=whole_recv.at[0],
+            device_id=(to % 2 * 4 + y, x * 8 + to // 2 * 2 + core), device_id_type=MESH)
+
+    def each(count, me, act):
+        def step(i, _):
+            act((me + i) % count)
+            return 0
+
+        lax.fori_loop(1, count, step, 0)
+
     yl = lax.broadcasted_iota(jnp.int32, (64, 256), 1) % 8
 
     def gradient(i, e):
@@ -415,7 +442,7 @@
         rest = jnp.where(yl < 2, g[0], jnp.where(yl < 4, g[1], jnp.where(yl < 6, g[2], g[3])))
         d1, d2 = jnp.where(yl % 2 == 0, rest, 0.0), jnp.where(yl % 2 == 1, rest, 0.0)
         for b, d in enumerate((d0, d1, d2)):
-            group, slot = divmod(9 * e + 3 * i + b, 4)
+            group, slot = divmod(6 * e + 3 * i + b if i < 2 else FIRST + 3 * e + b, 4)
             at = (slice(64 * group, 64 * group + 64), slice(256 * slot, 256 * slot + 256))
             top = d.astype(BF)
             dh[at] = top
@@ -424,6 +451,21 @@
     for e in range(3):
         gradient(0, e)
         gradient(1, e)
+    loads["bands"].wait()
+
+    def send_parts(first, end):
+        rows = slice(16 * first, 16 * end)
+        packed = dot(dh[rows], k["bands"][...]) + dot(dl[rows], k["bands"][...])
+        terms[first:end] = packed.reshape(end - first, 16, 128)
+
+        def send(to):
+            @pl.when((to >= first) & (to < end))
+            def _():
+                part_copy(to, mine).start()
+
+        each(32, mine, send)
+
+    send_parts(0, FIRST)
 
     @pl.when(core == 0)
     def _():
@@ -432,26 +474,7 @@
     lax.fori_loop(0, BANDS, forms_later, 0)
     for e in range(3):
         gradient(2, e)
-    loads["bands"].wait()
-    packed = dot(dh[...], k["bands"][...]) + dot(dl[...], k["bands"][...])
-    terms[0:28] = packed.reshape(28, 16, 128)
-
-    def layer_copy(source, target, send, recv, to, slot):
-        return pltpu.make_async_remote_copy(
-            src_ref=source, dst_ref=target.at[slot], send_sem=send.at[0], recv_sem=recv.at[0],
-            device_id=(z_lo * 4 + to // 2 % 4, to // 8 * 8 + z_hi * 2 + to % 2), device_id_type=MESH)
-
-    def part_copy(to, slot):
-        return layer_copy(terms.at[to], part_in, part_send, part_recv, to, slot)
-
-    def last_copy(to, slot):
-        return layer_copy(whole, gathered, last_send, last_recv, to, slot)
-
-    def whole_copy(to, slot):
-        return pltpu.make_async_remote_copy(
-            src_ref=part, dst_ref=whole_in.at[slot],
-            send_sem=whole_send.at[0], recv_sem=whole_recv.at[0],
-            device_id=(to % 2 * 4 + y, x * 8 + to // 2 * 2 + core), device_id_type=MESH)
+    send_parts(FIRST, 32)
 
     loads["weave"].wait()
 
@@ -471,14 +494,6 @@
             for zz in range(2):
                 vgrad[:, 2 * zz + parity, 16 * n : 16 * n + 16, :] = out[:, :, 128 * zz : 128 * zz + 128]
 
-    def each(count, me, act):
-        def step(i, _):
-            act((me + i) % count)
-            return 0
-
-        lax.fori_loop(1, count, step, 0)
-
-    each(32, mine, lambda to: part_copy(to, mine).start())
     part_in[mine] = terms[mine]
 
     @pl.when(core == 0)
@@ -550,7 +565,7 @@
     for g in range(GROUPS):
         total = jnp.transpose(gathered[4 * g : 4 * g + 4].astype(F32).reshape(64, 128))
         for slot in range(4):
-            if 4 * g + slot < len(TAPS):
+            if TAPS[4 * g + slot] is not None:
                 kgrad[TAPS[4 * g + slot]] = total[32 * slot : 32 * slot + 32]
     copies[2].start()
     for copy in copies:

time: 57.6 us -> 58.2 us (1.010)
  no operation moved by 1% of the time
where the time goes in v4:
time: 58.2 us; the launch traced here: 58.1 us
  Pallas kernels  57.4 us (99%)
  between operations  0.64 us (1%)
    pallas_call x1, Pallas kernels, shards(): pl.pallas_call(kernel, out_shape=held, in_specs=[anywhere] * (3 + NC), ou...  55.6 us
    pallas_call x1, Pallas kernels, shards(): pl.pallas_call(store, out_shape=outs, in_specs=[inside] * 3, out_specs=(a...  1.83 us

profile of v4, /device:TPU:1, one launch (start us, length us, event | category | flops | bytes accessed | tf_op | source)
XLA Modules:
  0.0 58.1 jit_solution(7152413807463086235)
XLA Ops:
  0.6 55.6 %shard_map.193 = (bf16[64,64,64]{2,1,0:T(8,128)(2,1)S(1)}, bf16[32,4,64,128]{3,2,1,0:T(8,128)(2,1)S(1)}, bf16[32,16,128]{2,1,0:T(8,128)(2,1)S(1)}) custom-call(bf16[32,4,64,128]{3,2,1,0:T(8,128)(2,1)} %bitcast.8, bf16[3,3,3,32,64]{4,3,2,1,0:T(8,128)(2,1)} %bitcast.13, bf16[64,64,64]{2,1,0:T(8,128)(2,1)} %bitcast.10, bf16[64,256]{1,0:T(8,128)(2,1)} %constant.30.clone.refs_3_, ...), custom_call_target="tpu_custom_call" | custom-call | flops 20000000000 | bytes 8388608 | tf_op jit(solution)/shard_map/pallas_call | solution.py:618
  56.3 1.8 %shard_map.194 = (bf16[64,64,64]{2,1,0:T(8,128)(2,1)}, bf16[32,4,64,128]{3,2,1,0:T(8,128)(2,1)}, f32[3,3,3,32,64]{4,3,2,1,0:T(8,128)}) custom-call(bf16[64,64,64]{2,1,0:T(8,128)(2,1)S(1)} %get-tuple-element.9.feat, bf16[32,4,64,128]{3,2,1,0:T(8,128)(2,1)S(1)} %get-tuple-element.10.vgrad, bf16[32,16,128]{2,1,0:T(8,128)(2,1)S(1)} %get-tuple-element.11.gathered), custom_call_target="tpu_custom_call" | custom-call | tf_op jit(solution)/shard_map/pallas_call | solution.py:637

commit v5 on v3

--- a/solution.py
+++ b/solution.py
@@ -492,21 +492,21 @@
         arrived(vc.at[0, 0:1232], cot_send)
 
     backward(0)
+    backward(1)
     arrived(part_in.at[0:31], part_recv)
     part[...] = functools.reduce(jnp.add, [part_in[i] for i in range(32)])
 
     each(8, z, lambda to: whole_copy(to, z).start())
     whole_in[z] = part[...]
     arrived(terms.at[0:31], part_send)
-    backward(1)
+    backward(2)
+    backward(3)
     arrived(whole_in.at[0:7], whole_recv)
     whole[...] = (functools.reduce(jnp.add, [whole_in[i] for i in range(8)]) * 0.125).astype(BF)
 
     each(32, mine, lambda to: last_copy(to, mine).start())
     gathered[mine] = whole[...]
     arrived(whole_in.at[0:7], whole_send)
-    backward(2)
-    backward(3)
 
     @pl.when(core == 0)
     def _():

time: 57.6 us -> 57.6 us (level)
  no operation moved by 1% of the time
where the time goes in v5:
time: 57.6 us; the launch traced here: 57.5 us
  Pallas kernels  56.9 us (99%)
  between operations  0.64 us (1%)
    pallas_call x1, Pallas kernels, shards(): pl.pallas_call(kernel, out_shape=held, in_specs=[anywhere] * (3 + NC), ou...  55 us
    pallas_call x1, Pallas kernels, shards(): pl.pallas_call(store, out_shape=outs, in_specs=[inside] * 3, out_specs=(a...  1.83 us

profile of v5, /device:TPU:1, one launch (start us, length us, event | category | flops | bytes accessed | tf_op | source)
XLA Modules:
  0.0 57.5 jit_solution(12411915557623940064)
XLA Ops:
  0.6 55.0 %shard_map.193 = (bf16[64,64,64]{2,1,0:T(8,128)(2,1)S(1)}, bf16[32,4,64,128]{3,2,1,0:T(8,128)(2,1)S(1)}, bf16[32,16,128]{2,1,0:T(8,128)(2,1)S(1)}) custom-call(bf16[32,4,64,128]{3,2,1,0:T(8,128)(2,1)} %bitcast.8, bf16[3,3,3,32,64]{4,3,2,1,0:T(8,128)(2,1)} %bitcast.13, bf16[64,64,64]{2,1,0:T(8,128)(2,1)} %bitcast.10, bf16[64,256]{1,0:T(8,128)(2,1)} %constant.30.clone.refs_3_, ...), custom_call_target="tpu_custom_call" | custom-call | flops 20000000000 | bytes 8388608 | tf_op jit(solution)/shard_map/pallas_call | solution.py:603
  55.7 1.8 %shard_map.194 = (bf16[64,64,64]{2,1,0:T(8,128)(2,1)}, bf16[32,4,64,128]{3,2,1,0:T(8,128)(2,1)}, f32[3,3,3,32,64]{4,3,2,1,0:T(8,128)}) custom-call(bf16[64,64,64]{2,1,0:T(8,128)(2,1)S(1)} %get-tuple-element.9.feat, bf16[32,4,64,128]{3,2,1,0:T(8,128)(2,1)S(1)} %get-tuple-element.10.vgrad, bf16[32,16,128]{2,1,0:T(8,128)(2,1)S(1)} %get-tuple-element.11.gathered), custom_call_target="tpu_custom_call" | custom-call | tf_op jit(solution)/shard_map/pallas_call | solution.py:622
